TPU v7x, 256 devices: a whole 4x4x8 slice. The times are simulated.
256 devices in a mesh: ka: 8 (over y, x_hi), ta: 32 (over x_lo, z, core).
Axes of the slice: x: 4 (x_hi: 2, x_lo: 2; x = x_hi * 2 + x_lo), y: 4, z: 8, core: 2. Of those that a mesh axis runs over, the one named last changes fastest.
Arguments:
- green_time: bfloat16 [2, 144, 2048, 128], P(None, 'ka', 'ta'), may hold values from -6 to 6
- screened_time: bfloat16 [2, 144, 2048, 128], P(None, 'ka', 'ta'), may hold values from -0.5 to 0.5
- panel_orbitals: bfloat16 [2, 144, 128, 128], P(None, 'ka'), may hold values from -0.1796875 to 0.1796875
- column_orbitals: bfloat16 [2, 144, 2048, 128], P(None, 'ka', 'ta'), may hold values from -0.1796875 to 0.1796875
Outputs:
- band_sigma: float32 [2, 2, 144, 128, 128], P(None, None, 'ka', None, 'ta')
All inputs are finite; a program needn't handle non-finite values.
Results may differ from a plain program's by a relative error of at most 0.0049.
Values may be sent and summed in bfloat16 or wider, within the bound.
A program may use at most 64 MiB of HBM per device.

v0:
```python
import jax
import jax.numpy as jnp
from jax import lax
from jax.sharding import PartitionSpec as P

LA = 6
LC = 4
NK = 144


def lattice_table():
    cells = jnp.arange(NK, dtype=jnp.int32)
    first = cells // (LA * LC)
    second = cells // LC % LA
    third = cells % LC
    outer = (first[:, None] * first[None, :] + second[:, None] * second[None, :]) % LA
    inner = third[:, None] * third[None, :] % LC
    turns = (outer * LC + inner * LA) % (LA * LC)
    angle = turns.astype(jnp.float32) * (2.0 * jnp.pi / (LA * LC))
    return jnp.stack([jnp.cos(angle), -jnp.sin(angle)])


def body(green_time, screened_time, panel_orbitals, column_orbitals):
    table = lattice_table()
    local_cells = green_time.shape[1]
    product = (green_time.astype(jnp.float32) * screened_time.astype(jnp.float32)).astype(
        jnp.bfloat16
    )
    anchor = lax.axis_index("ka") * local_cells
    columns = lax.dynamic_slice_in_dim(table, anchor, local_cells, 2)
    widened = product.astype(jnp.float32)
    summed = lax.psum_scatter(
        jnp.einsum("ckr,trnm->kctnm", columns, widened, precision=lax.Precision.HIGHEST),
        "ka",
        scatter_dimension=0,
        tiled=True,
    )
    spectral = jnp.transpose(summed.astype(jnp.bfloat16), (2, 1, 0, 3, 4))
    s_real = spectral[:, 0]
    s_imag = spectral[:, 1]
    p_real = panel_orbitals[0]
    p_imag = panel_orbitals[1]
    wide_type = jnp.float32
    h_real = jnp.einsum(
        "kmi,tknm->tkni", p_real, s_real, preferred_element_type=wide_type
    ) + jnp.einsum("kmi,tknm->tkni", p_imag, s_imag, preferred_element_type=wide_type)
    h_imag = jnp.einsum(
        "kmi,tknm->tkni", p_real, s_imag, preferred_element_type=wide_type
    ) - jnp.einsum("kmi,tknm->tkni", p_imag, s_real, preferred_element_type=wide_type)
    half_real = h_real.astype(jnp.bfloat16)
    half_imag = h_imag.astype(jnp.bfloat16)
    c_real = column_orbitals[0]
    c_imag = column_orbitals[1]
    z_real = jnp.einsum(
        "tkni,knj->tkij", half_real, c_real, preferred_element_type=wide_type
    ) - jnp.einsum("tkni,knj->tkij", half_imag, c_imag, preferred_element_type=wide_type)
    z_imag = jnp.einsum(
        "tkni,knj->tkij", half_real, c_imag, preferred_element_type=wide_type
    ) + jnp.einsum("tkni,knj->tkij", half_imag, c_real, preferred_element_type=wide_type)
    partial_bands = jnp.stack([z_real, z_imag], axis=1)
    return lax.psum_scatter(partial_bands, "ta", scatter_dimension=4, tiled=True)


def solution(mesh):
    return jax.shard_map(
        body,
        mesh=mesh,
        in_specs=(
            P(None, "ka", "ta", None),
            P(None, "ka", "ta", None),
            P(None, "ka", None, None),
            P(None, "ka", "ta", None),
        ),
        out_specs=P(None, None, "ka", None, "ta"),
        check_vma=False,
    )
```

profile of v0, /device:TPU:1, one launch (start us, length us, event | category | flops | bytes accessed | tf_op | source)
XLA Modules:
  0.0 518.3 jit_solution(7017265398429526672)
XLA Ops:
  6.6 1.5 fusion.6
  8.0 0.8 sine_negate_fusion
  8.9 7.6 %convolution_bitcast_fusion = f32[144,2,2,64,128]{4,0,1,3,2:T(8,128)S(1)} fusion(bf16[2,18,64,128,1]{3,2,1,0,4:T(8,128)(2,1)S(1)} %fusion.6, s32[]{:T(128)S(6)} %select_n.122, f32[1,144,144]{1,2,0:T(8,128)S(1)} %get-tuple-element.6, f32[1,144,144]{1,2,0:T(8,128)S(1)} %get-tuple-element.5), kind=kOutput, calls=%fused_computation | convolution fusion | flops 1019221056 | bytes 19630084 | tf_op jit(solution)/shard_map/ckr,trnm->kctnm/dot_general | solution.py:33
  16.4 21.9 %copy.12 = f32[144,2,2,64,128]{4,3,2,1,0:T(8,128)} copy(f32[144,2,2,64,128]{4,0,1,3,2:T(8,128)S(1)} %convolution_bitcast_fusion) | data formatting | bytes 37748736 | tf_op jit(solution)/shard_map/ckr,trnm->kctnm/transpose | solution.py:33
  38.4 0.0 reduce-scatter.2.cloned.1.call-update
  38.4 0.0 all-reduce.3.cloned.1.call-start
  38.5 216.3 %reduce-scatter.2.cloned.1.call-done = f32[18,2,2,64,128]{4,3,2,1,0:T(8,128)} async-done(((f32[144,2,2,64,128]{4,3,2,1,0:T(8,128)}), f32[18,2,2,64,128]{4,3,2,1,0:T(8,128)}) %reduce-scatter.2.cloned.1.call-update) | async-done | bytes 2359312 | tf_op jit(solution)/shard_map/reduce_scatter | solution.py:32
  254.8 1.9 copy.29
  256.7 0.3 fusion.9
  257.1 0.3 fusion.11
  257.4 0.3 fusion.3
  257.7 0.7 copy-done.1
  258.5 0.5 fusion.18
  259.0 0.5 fusion.20
  259.5 0.3 fusion.2
  259.8 0.5 subtract_bitcast_fusion
  260.4 0.5 add_bitcast_fusion
  260.9 2.7 pad_maximum_fusion
  263.6 8.1 %copy.14 = f32[2,2,18,128,128]{3,1,2,0,4:T(2,128)} copy(f32[2,2,18,128,128]{4,3,0,2,1:T(8,128)} %pad_maximum_fusion) | data formatting | bytes 9437184 | tf_op jit(solution)/shard_map/stack | solution.py:60
  271.8 0.6 copy-done.2
  272.4 0.6 dynamic-slice
  273.7 236.1 %all-reduce.3.cloned.1.call-done = f32[2,2,18,128,128]{3,1,2,0,4:T(2,128)} async-done(((f32[2,2,18,128,128]{3,1,2,0,4:T(2,128)}), f32[2,2,18,128,128]{3,1,2,0,4:T(2,128)}) %all-reduce.3.cloned.1.call-update) | async-done | bytes 4718608
  509.8 0.9 constant_dynamic-slice_fusion
  510.7 0.7 copy.15
  (8 shorter events, 0.0 us)
Async XLA Ops:
  6.5 248.3 %reduce-scatter.2.cloned.1.call-start = ((), (), s32[]{:S(2)}) async-start(), calls=%async_computation.1 | async-start | bytes 21233664 | tf_op jit(solution)/shard_map/reduce_scatter | solution.py:32
  38.4 218.3 %copy-start = (bf16[2,18,128,128]{3,2,1,0:T(8,128)(2,1)S(1)}, bf16[2,18,128,128]{3,2,1,0:T(8,128)(2,1)}, u32[]{:S(2)}) copy-start(bf16[2,18,128,128]{3,2,1,0:T(8,128)(2,1)} %param.6) | copy-start | bytes 3538948
  38.4 471.4 %all-reduce.3.cloned.1.call-start = ((), (), s32[]{:S(2)}) async-start(), calls=%async_computation.2 | async-start | bytes 9437184
  257.4 1.1 copy-start.1
  271.8 0.7 copy-start.2
Sparse Core Ops, SparseCore 0:
  38.5 216.2 reduce-scatter.1
  271.9 237.8 all-reduce.2
where the time goes:
time: 519 us; the launch traced here: 518 us
  waiting for transfers between devices  453 us (87%)
  local copies, waits for them, and re-layouts  35.6 us (7%)
  between operations  14.2 us (3%)
  matrix products  10.9 us (2%)
    unnamed x3, waiting for transfers between devices  236 us
    reduce_scatter x1, waiting for transfers between devices, body(): lax.psum_scatter(jnp.einsum('ckr,trnm->kctnm', columns, widened, precisio...  216 us
    transpose x1, local copies, waits for them, and re-layouts, body(): jnp.einsum('ckr,trnm->kctnm', columns, widened, precision=lax.Precision.H...  21.9 us
  transfers between devices with their start and end apart: 2, of which 2 were waited for; matrix products, arithmetic and copies ran while one was open for 0% of the time, Pallas kernels for 0%

commit v1 on v0

v1 whole, which is shorter than its diff:
```python
import jax
import jax.numpy as jnp
from jax import lax
from jax.experimental import pallas as pl
from jax.experimental.pallas import tpu as pltpu
from jax.sharding import PartitionSpec as P

MESH = pl.DeviceIdType.MESH
BF = jnp.bfloat16
F32 = jnp.float32
NY, NX, NZ = 4, 4, 8
NA = 8
LA, LC = 6, 4
NK = 144
KB = 18
KH = 9
NCH = 3
KC = KH // NCH
SUB = 16
HALF_SQRT3 = 0.8660254037844386


def real_dft6(x):
    e0, e1, e2 = x[0] + x[3], x[1] + x[4], x[2] + x[5]
    o0, o1, o2 = x[0] - x[3], x[1] - x[4], x[2] - x[5]
    es = e1 + e2
    od = o1 - o2
    x1 = (o0 + 0.5 * od, -HALF_SQRT3 * (o1 + o2))
    x2 = (e0 - 0.5 * es, -HALF_SQRT3 * (e1 - e2))
    return e0 + es, o0 - od, x1, x2


def complex_dft6(re, im):
    a0, a3, a1, a2 = real_dft6(re)
    b0, b3, b1, b2 = real_dft6(im)
    return (
        (a0, b0),
        (a1[0] - b1[1], a1[1] + b1[0]),
        (a2[0] - b2[1], a2[1] + b2[0]),
        (a3, b3),
        (a2[0] + b2[1], b2[0] - a2[1]),
        (a1[0] + b1[1], b1[0] - a1[1]),
    )


def lattice_dft(cells, stage, spectral):
    def inner(r1, carry):
        block = cells[pl.ds(r1 * 24, 24)].astype(F32)
        zero, two, one_re, one_im = [], [], [], []
        for r2 in range(LA):
            x0, x1, x2, x3 = (block[4 * r2 + j] for j in range(LC))
            s02, s13 = x0 + x2, x1 + x3
            zero.append(s02 + s13)
            two.append(s02 - s13)
            one_re.append(x0 - x2)
            one_im.append(x3 - x1)
        for base, values in ((0, zero), (6, two)):
            v0, v3, v1, v2 = real_dft6(values)
            for slot, value in enumerate((v0, v3, v1[0], v1[1], v2[0], v2[1])):
                stage[r1, base + slot] = value
        for k2, pair in enumerate(complex_dft6(one_re, one_im)):
            stage[r1, 12 + 2 * k2] = pair[0]
            stage[r1, 13 + 2 * k2] = pair[1]
        return carry

    lax.fori_loop(0, LA, inner, 0)

    def put(k, re, im):
        spectral[0, k] = re.astype(BF)
        spectral[1, k] = im.astype(BF)

    def outer_complex(slot, k2, k3):
        re = [stage[r1, slot] for r1 in range(LA)]
        im = [stage[r1, slot + 1] for r1 in range(LA)]
        there = (LA - k2) % LA * LC + (LC - k3) % LC
        for k1, pair in enumerate(complex_dft6(re, im)):
            put(k1 * 24 + k2 * LC + k3, pair[0], pair[1])
            put((LA - k1) % LA * 24 + there, pair[0], -pair[1])

    def third_one(k2, carry):
        outer_complex(12 + 2 * k2, k2, 1)
        return carry

    lax.fori_loop(0, LA, third_one, 0)

    def third_even(i, carry):
        outer_complex(6 * (i // 2) + 2 + 2 * (i % 2), 1 + i % 2, 2 * (i // 2))
        return carry

    lax.fori_loop(0, 4, third_even, 0)

    def all_real(i, carry):
        k2, k3 = 3 * (i % 2), 2 * (i // 2)
        slot = 6 * (i // 2) + i % 2
        x0, x3, x1, x2 = real_dft6([stage[r1, slot] for r1 in range(LA)])
        base = k2 * LC + k3
        none = jnp.zeros_like(x0)
        put(base, x0, none)
        put(24 + base, x1[0], x1[1])
        put(48 + base, x2[0], x2[1])
        put(72 + base, x3, none)
        put(96 + base, x2[0], -x2[1])
        put(120 + base, x1[0], -x1[1])
        return carry

    lax.fori_loop(0, 4, all_real, 0)


def placing_tables():
    row = lax.broadcasted_iota(jnp.int32, (256, 256), 0)
    lane = lax.broadcasted_iota(jnp.int32, (256, 256), 1)
    j = ((row >> 4) & 1) * 64 + (row >> 5) * 8 + ((row >> 3) & 1) * 4 + (row & 3)
    part = (row >> 2) & 1
    first = jnp.where(lane == part * 128 + j, 1.0, 0.0)
    sign = jnp.where(part == 0, -1.0, 1.0)
    second = jnp.where(lane == (1 - part) * 128 + j, sign, 0.0)
    return first.astype(BF), second.astype(BF)


def kernel(
    green, screened, panel, column, out,
    g_buf, w_buf, product, cells, stage, spectral, sigma, pan, cols, placing, lhs, bands, to_send, received, quarter,
    load_sem, col_local, col_send, col_recv, p1_send, p1_recv, p2_send, p2_recv, r_send, r_recv, f_send, f_recv,
):
    ka = lax.axis_index("ka")
    ta = lax.axis_index("ta")
    y, xh = ka // 2, ka % 2
    xl, z, core = ta // (2 * NZ), ta // 2 % NZ, ta % 2
    x = 2 * xh + xl

    def device(y_, x_, z_, core_):
        return (y_ * 2 + x_ // 2, (x_ % 2 * NZ + z_) * 2 + core_)

    loads = [
        pltpu.make_async_copy(green, g_buf, load_sem.at[0]),
        pltpu.make_async_copy(screened, w_buf, load_sem.at[1]),
        pltpu.make_async_copy(panel.at[:, pl.ds(KH * xl, KH)], pan, load_sem.at[2]),
        pltpu.make_async_copy(column.at[:, pl.ds(KH * xl, KH)], cols.at[xl, core], col_local),
    ]
    for load in loads:
        load.start()

    barrier = pltpu.get_barrier_semaphore()

    def greet_plane(d, carry):
        there = device((y + d // 8) % NY, (x + d // 2 % NX) % NX, z, (core + d % 2) % 2)
        pl.semaphore_signal(barrier, inc=1, device_id=there, device_id_type=MESH)
        return carry

    lax.fori_loop(1, 32, greet_plane, 0)

    def greet_z(d, carry):
        pl.semaphore_signal(barrier, inc=1, device_id=device(y, x, (z + d) % NZ, core), device_id_type=MESH)
        return carry

    lax.fori_loop(1, NZ, greet_z, 0)

    loads[0].wait()
    loads[1].wait()

    def multiply(r, carry):
        for t in range(2):
            product[t, r] = (g_buf[t, r].astype(F32) * w_buf[t, r].astype(F32)).astype(BF)
        return carry

    lax.fori_loop(0, KB, multiply, 0)
    pl.semaphore_wait(barrier, 31 + NZ - 1)

    def send_cells(i, carry):
        sub, t = i // 2, i % 2
        there = 4 * core + sub
        pltpu.make_async_remote_copy(
            src_ref=product.at[t, :, pl.ds(pl.multiple_of(sub * SUB, SUB), SUB)],
            dst_ref=cells.at[pl.ds(ka * KB, KB)],
            send_sem=p1_send,
            recv_sem=p1_recv,
            device_id=device(there // 2, 2 * (there % 2) + 1 - xl, z, t),
            device_id_type=MESH,
        ).start()
        return carry

    lax.fori_loop(0, 8, send_cells, 0)

    to_core = pltpu.make_async_remote_copy(
        src_ref=column.at[:, pl.ds(KH * xl, KH)],
        dst_ref=cols.at[xl, core],
        send_sem=col_send.at[0],
        recv_sem=col_recv.at[0],
        device_id=device(y, x, z, 1 - core),
        device_id_type=MESH,
    )
    to_x = pltpu.make_async_remote_copy(
        src_ref=column.at[:, pl.ds(KH * (1 - xl), KH)],
        dst_ref=cols.at[xl, core],
        send_sem=col_send.at[1],
        recv_sem=col_recv.at[1],
        device_id=device(y, 2 * xh + 1 - xl, z, core),
        device_id_type=MESH,
    )
    forward = pltpu.make_async_remote_copy(
        src_ref=cols.at[1 - xl, core],
        dst_ref=cols.at[1 - xl, core],
        send_sem=col_send.at[2],
        recv_sem=col_recv.at[2],
        device_id=device(y, x, z, 1 - core),
        device_id_type=MESH,
    )
    to_core.start()
    to_x.start()

    first, second = placing_tables()
    placing[0:256] = first
    placing[256:512] = second

    pltpu.make_async_copy(cells, cells, p1_recv).wait()
    lattice_dft(cells, stage, spectral)

    mine = (1 - xl) * NA + ka
    for chunk in range(NCH):
        own_k = (ka * 2 + xl) * KH + chunk * KC
        pltpu.make_async_copy(
            spectral.at[:, pl.ds(own_k, KC)], sigma.at[chunk, mine], p2_recv.at[chunk]
        ).start()

        def send_points(d, carry, chunk=chunk):
            y_, x_ = (y + d // NX) % NY, (x + d % NX) % NX
            k = (y_ * NX + x_) * KH + chunk * KC
            pltpu.make_async_remote_copy(
                src_ref=spectral.at[:, pl.ds(k, KC)],
                dst_ref=sigma.at[chunk, mine],
                send_sem=p2_send,
                recv_sem=p2_recv.at[chunk],
                device_id=device(y_, x_, z, core),
                device_id_type=MESH,
            ).start()
            return carry

        lax.fori_loop(1, NY * NX, send_points, 0)

    to_x.wait_recv()
    forward.start()
    loads[2].wait()
    loads[3].wait()
    to_core.wait_recv()
    forward.wait_recv()

    def place(k, carry):
        parts = [
            jnp.concatenate([cols[a, b, part, k] for a in range(2) for b in range(2)], axis=0)
            for part in range(2)
        ]
        both = jnp.concatenate(parts, axis=1)
        placed = lax.dot_general(
            placing[...], both, (((1,), (1,)), ((), ())), preferred_element_type=F32
        ).astype(BF)
        lhs[k] = jnp.concatenate([placed[0:256], placed[256:512]], axis=1)
        return carry

    lax.fori_loop(0, KH, place, 0)

    for chunk in range(NCH):
        pltpu.make_async_copy(sigma.at[chunk], sigma.at[chunk], p2_recv.at[chunk]).wait()

        def contract(kk, carry, chunk=chunk):
            k = chunk * KC + kk
            s = jnp.concatenate(
                [sigma[chunk, :, part, kk].reshape(256, 128) for part in range(2)], axis=1
            )
            p_re, p_im = pan[0, k], pan[1, k]
            weights = jnp.concatenate(
                [jnp.concatenate([p_re, -p_im], axis=1), jnp.concatenate([p_im, p_re], axis=1)], axis=0
            )
            half = jnp.dot(s, weights, preferred_element_type=F32).astype(BF)
            stacked = jnp.concatenate([half[:, 0:128], half[:, 128:256]], axis=0)
            band = jnp.dot(lhs[k], stacked, preferred_element_type=F32)
            bands[k] = band
            to_send[k] = band.astype(BF).reshape(NZ, 32, 128)
            return carry

        lax.fori_loop(0, KC, contract, 0)

        def send_bands(d, carry, chunk=chunk):
            z_ = (z + d) % NZ
            pltpu.make_async_remote_copy(
                src_ref=to_send.at[pl.ds(chunk * KC, KC), z_],
                dst_ref=received.at[chunk, z],
                send_sem=r_send,
                recv_sem=r_recv.at[chunk],
                device_id=device(y, x, z_, core),
                device_id_type=MESH,
            ).start()
            return carry

        lax.fori_loop(1, NZ, send_bands, 0)

    for chunk in range(NCH):
        some = received.at[chunk, pl.ds(0, NZ - 1)]
        pltpu.make_async_copy(some, some, r_recv.at[chunk]).wait()

        def add_up(kk, carry, chunk=chunk):
            k = chunk * KC + kk
            total = bands[k, pl.ds(pl.multiple_of(z * 32, 32), 32)]
            for d in range(1, NZ):
                total = total + received[chunk, (z + d) % NZ, kk].astype(F32)
            for g in range(4):
                quarter[g, k] = total[8 * g : 8 * g + 8]
            return carry

        lax.fori_loop(0, KC, add_up, 0)

    for d in range(1, 4):
        xl_, core_ = (xl + d // 2) % 2, (core + d % 2) % 2
        pltpu.make_async_remote_copy(
            src_ref=quarter.at[2 * xl_ + core_],
            dst_ref=out.at[core, pl.ds(KH * xl, KH)],
            send_sem=f_send,
            recv_sem=f_recv,
            device_id=device(y, 2 * xh + xl_, z, core_),
            device_id_type=MESH,
        ).start()
    out[core, pl.ds(KH * xl, KH)] = quarter[2 * xl + core]

    three = quarter.at[pl.ds(0, 3)]
    pltpu.make_async_copy(three, three, f_recv).wait()

    pltpu.make_async_copy(cells, cells, p1_send).wait()
    to_core.wait_send()
    to_x.wait_send()
    forward.wait_send()
    others = sigma.at[:, pl.ds(0, NY * NX - 1)]
    pltpu.make_async_copy(others, others, p2_send).wait()
    others = received.at[:, pl.ds(0, NZ - 1)]
    pltpu.make_async_copy(others, others, r_send).wait()
    pltpu.make_async_copy(three, three, f_send).wait()


def body(green, screened, panel, column):
    dma = pltpu.SemaphoreType.DMA
    bands = pl.pallas_call(
        kernel,
        out_shape=jax.ShapeDtypeStruct((2, KB, 8, 128), F32),
        in_specs=[pl.BlockSpec(memory_space=pltpu.HBM)] * 4,
        out_specs=pl.BlockSpec(memory_space=pltpu.VMEM),
        scratch_shapes=[
            pltpu.VMEM((2, KB, 64, 128), BF),
            pltpu.VMEM((2, KB, 64, 128), BF),
            pltpu.VMEM((2, KB, 64, 128), BF),
            pltpu.VMEM((NK, SUB, 128), BF),
            pltpu.VMEM((LA, 24, SUB, 128), F32),
            pltpu.VMEM((2, NK, SUB, 128), BF),
            pltpu.VMEM((NCH, 16, 2, KC, SUB, 128), BF),
            pltpu.VMEM((2, KH, 128, 128), BF),
            pltpu.VMEM((2, 2, 2, KH, 64, 128), BF),
            pltpu.VMEM((512, 256), BF),
            pltpu.VMEM((KH, 256, 512), BF),
            pltpu.VMEM((KH, 256, 128), F32),
            pltpu.VMEM((KH, NZ, 32, 128), BF),
            pltpu.VMEM((NCH, NZ, KC, 32, 128), BF),
            pltpu.VMEM((4, KH, 8, 128), F32),
            dma((3,)),
            dma,
            dma((3,)),
            dma((3,)),
            dma,
            dma,
            dma,
            dma((NCH,)),
            dma,
            dma((NCH,)),
            dma,
            dma,
        ],
        compiler_params=pltpu.CompilerParams(
            collective_id=0, has_side_effects=True, vmem_limit_bytes=60 * 1024 * 1024
        ),
    )(green, screened, panel, column)
    return jnp.transpose(bands.reshape(2, KB, 2, 4, 128), (0, 2, 1, 4, 3))


def solution(mesh):
    return jax.shard_map(
        body,
        mesh=mesh,
        in_specs=(
            P(None, "ka", "ta", None),
            P(None, "ka", "ta", None),
            P(None, "ka", None, None),
            P(None, "ka", "ta", None),
        ),
        out_specs=P(None, None, "ka", None, "ta"),
        check_vma=False,
    )
```

time: 519 us -> 54.7 us (0.11)
  waiting for transfers between devices: 453 us -> 0 us
  Pallas kernels: 0 us -> 53 us
  local copies, waits for them, and re-layouts: 35.6 us -> 1.6 us
  between operations: 14.2 us -> 0.01 us
  matrix products: 10.9 us -> 0 us
    unnamed x3 -> x0, waiting for transfers between devices: 236 us -> none
    reduce_scatter x1 -> x0, waiting for transfers between devices: 216 us -> none  [body(): lax.psum_scatter(jnp.einsum('ckr,trnm->kctnm', columns, widened, precisio...]
    pallas_call x0 -> x1, Pallas kernels: none -> 53 us  [body(): pl.pallas_call(kernel, out_shape=jax.ShapeDtypeStruct((2, KB, 8, 128), F3...]
    transpose x1 -> x0, local copies, waits for them, and re-layouts: 21.9 us -> none  [body(): jnp.einsum('ckr,trnm->kctnm', columns, widened, precision=lax.Precision.H...]
    dot_general x9 -> x0, matrix products: 10.9 us -> none  [the longest x1 7.57 us: body(): jnp.einsum('ckr,trnm->kctnm', columns, widened, precision=lax.Precision.H...]
    another operation x1 -> x0, local copies, waits for them, and re-layouts: 8.14 us -> none  [body(): partial_bands = jnp.stack([z_real, z_imag], axis=1)]
  transfers between devices with their start and end apart: 2 -> 0, of which waited for: 2 -> 0; matrix products, arithmetic and copies ran while one was open for 0% -> 0% of each run, Pallas kernels for 0% -> 0%
where the time goes in v1:
time: 54.7 us; the launch traced here: 54.6 us
  Pallas kernels  53 us (97%)
  local copies, waits for them, and re-layouts  1.6 us (3%)
    pallas_call x1, Pallas kernels, body(): pl.pallas_call(kernel, out_shape=jax.ShapeDtypeStruct((2, KB, 8, 128), F3...  53 us
    reshape x1, local copies, waits for them, and re-layouts, body(): return jnp.transpose(bands.reshape(2, KB, 2, 4, 128), (0, 2, 1, 4, 3))  1.6 us

profile of v1, /device:TPU:1, one launch (start us, length us, event | category | flops | bytes accessed | tf_op | source)
XLA Modules:
  0.0 54.6 jit_solution(101961241671159142)
XLA Ops:
  0.0 53.0 %shard_map.46 = f32[2,18,8,128]{3,2,1,0:T(8,128)} custom-call(bf16[2,18,64,128]{3,2,1,0:T(8,128)(2,1)} %green.1, bf16[2,18,64,128]{3,2,1,0:T(8,128)(2,1)} %screened.1, bf16[2,18,128,128]{3,2,1,0:T(8,128)(2,1)} %panel.1, bf16[2,18,64,128]{3,2,1,0:T(8,128)(2,1)} %column.1), custom_call_target="tpu_custom_call" | custom-call | tf_op jit(solution)/shard_map/pallas_call | solution.py:339
  53.0 1.6 %copy.7 = f32[2,18,2,4,128]{4,3,1,2,0:T(4,128)} copy(f32[2,18,2,4,128]{4,3,2,1,0:T(4,128)} %bitcast.4) | data formatting | bytes 294912 | tf_op jit(solution)/shard_map/reshape | solution.py:377

commit v2 on v1

v2 whole, which is shorter than its diff:
```python
import jax
import jax.numpy as jnp
from jax import lax
from jax.experimental import pallas as pl
from jax.experimental.pallas import tpu as pltpu
from jax.sharding import PartitionSpec as P

MESH = pl.DeviceIdType.MESH
BF = jnp.bfloat16
F32 = jnp.float32
NY, NX, NZ = 4, 4, 8
NA = 8
LA, LC = 6, 4
NK = 144
KB = 18
KH = 9
CHUNKS = (2, 2, 2, 1, 2)
STARTS = tuple(sum(CHUNKS[:i]) for i in range(len(CHUNKS)))
LAST = len(CHUNKS) - 1
EARLY = KH - CHUNKS[LAST]
AHEAD = 3
FAR_FIRST = sorted(
    ((dy, dx) for dy in range(NY) for dx in range(NX) if dy or dx),
    key=lambda d: -min(d[0], NY - d[0]) - min(d[1], NX - d[1]),
)
SUB = 16
HALF_SQRT3 = 0.8660254037844386


def real_dft6(x):
    e0, e1, e2 = x[0] + x[3], x[1] + x[4], x[2] + x[5]
    o0, o1, o2 = x[0] - x[3], x[1] - x[4], x[2] - x[5]
    es = e1 + e2
    od = o1 - o2
    x1 = (o0 + 0.5 * od, -HALF_SQRT3 * (o1 + o2))
    x2 = (e0 - 0.5 * es, -HALF_SQRT3 * (e1 - e2))
    return e0 + es, o0 - od, x1, x2


def complex_dft6(re, im):
    a0, a3, a1, a2 = real_dft6(re)
    b0, b3, b1, b2 = real_dft6(im)
    return (
        (a0, b0),
        (a1[0] - b1[1], a1[1] + b1[0]),
        (a2[0] - b2[1], a2[1] + b2[0]),
        (a3, b3),
        (a2[0] + b2[1], b2[0] - a2[1]),
        (a1[0] + b1[1], b1[0] - a1[1]),
    )


def lattice_dft(cells, stage, spectral):
    def inner(r1, carry):
        block = cells[pl.ds(r1 * 24, 24)].astype(F32)
        zero, two, one_re, one_im = [], [], [], []
        for r2 in range(LA):
            x0, x1, x2, x3 = (block[4 * r2 + j] for j in range(LC))
            s02, s13 = x0 + x2, x1 + x3
            zero.append(s02 + s13)
            two.append(s02 - s13)
            one_re.append(x0 - x2)
            one_im.append(x3 - x1)
        for base, values in ((0, zero), (6, two)):
            v0, v3, v1, v2 = real_dft6(values)
            for slot, value in enumerate((v0, v3, v1[0], v1[1], v2[0], v2[1])):
                stage[r1, base + slot] = value
        for k2, pair in enumerate(complex_dft6(one_re, one_im)):
            stage[r1, 12 + 2 * k2] = pair[0]
            stage[r1, 13 + 2 * k2] = pair[1]
        return carry

    lax.fori_loop(0, LA, inner, 0)

    def put(k, re, im):
        spectral[0, k] = re.astype(BF)
        spectral[1, k] = im.astype(BF)

    def outer_complex(slot, k2, k3):
        re = [stage[r1, slot] for r1 in range(LA)]
        im = [stage[r1, slot + 1] for r1 in range(LA)]
        there = (LA - k2) % LA * LC + (LC - k3) % LC
        for k1, pair in enumerate(complex_dft6(re, im)):
            put(k1 * 24 + k2 * LC + k3, pair[0], pair[1])
            put((LA - k1) % LA * 24 + there, pair[0], -pair[1])

    def third_one(k2, carry):
        outer_complex(12 + 2 * k2, k2, 1)
        return carry

    lax.fori_loop(0, LA, third_one, 0)

    def third_even(i, carry):
        outer_complex(6 * (i // 2) + 2 + 2 * (i % 2), 1 + i % 2, 2 * (i // 2))
        return carry

    lax.fori_loop(0, 4, third_even, 0)

    def all_real(i, carry):
        k2, k3 = 3 * (i % 2), 2 * (i // 2)
        slot = 6 * (i // 2) + i % 2
        x0, x3, x1, x2 = real_dft6([stage[r1, slot] for r1 in range(LA)])
        base = k2 * LC + k3
        none = jnp.zeros_like(x0)
        put(base, x0, none)
        put(24 + base, x1[0], x1[1])
        put(48 + base, x2[0], x2[1])
        put(72 + base, x3, none)
        put(96 + base, x2[0], -x2[1])
        put(120 + base, x1[0], -x1[1])
        return carry

    lax.fori_loop(0, 4, all_real, 0)


def placing_tables():
    row = lax.broadcasted_iota(jnp.int32, (256, 256), 0)
    lane = lax.broadcasted_iota(jnp.int32, (256, 256), 1)
    j = ((row >> 4) & 1) * 64 + (row >> 5) * 8 + ((row >> 3) & 1) * 4 + (row & 3)
    part = (row >> 2) & 1
    first = jnp.where(lane == part * 128 + j, 1.0, 0.0)
    sign = jnp.where(part == 0, -1.0, 1.0)
    second = jnp.where(lane == (1 - part) * 128 + j, sign, 0.0)
    return first.astype(BF), second.astype(BF)


def kernel(
    green, screened, panel, column, out,
    g_buf, w_buf, product, cells, stage, spectral, sigma, pan, cols, placing, lhs, to_send, received, quarter,
    to_owner, from_all, final,
    load_sem, col_local, col_send, col_recv, p1_send, p1_recv, p2_send, p2_recv, r_send, r_recv, l_send, l_recv, f_send, f_recv, s_send, s_recv,
):
    ka = lax.axis_index("ka")
    ta = lax.axis_index("ta")
    y, xh = ka // 2, ka % 2
    xl, z, core = ta // (2 * NZ), ta // 2 % NZ, ta % 2
    x = 2 * xh + xl

    def device(y_, x_, z_, core_):
        return (y_ * 2 + x_ // 2, (x_ % 2 * NZ + z_) * 2 + core_)

    barrier = pltpu.get_barrier_semaphore()

    def greet(there):
        pl.semaphore_signal(barrier, inc=1, device_id=there, device_id_type=MESH)

    for dy, dx in FAR_FIRST:
        greet(device((y + dy) % NY, (x + dx) % NX, z, core))
    for dy in (2, 1, 3, 0):
        for dx in (1, 3):
            greet(device((y + dy) % NY, (x + dx) % NX, z, 1 - core))
    greet(device(y, x, z, 1 - core))
    for dz in (4, 3, 5, 2, 6, 1, 7):
        greet(device(y, x, (z + dz) % NZ, core))

    loads = [
        pltpu.make_async_copy(green, g_buf, load_sem.at[0]),
        pltpu.make_async_copy(screened, w_buf, load_sem.at[1]),
        pltpu.make_async_copy(panel.at[:, pl.ds(KH * xl, KH)], pan, load_sem.at[2]),
        pltpu.make_async_copy(column.at[:, pl.ds(KH * xl, KH)], cols.at[0, core], col_local),
    ]
    for load in loads:
        load.start()

    loads[0].wait()
    loads[1].wait()

    def multiply(r, carry):
        for t in range(2):
            product[t, r] = (g_buf[t, r].astype(F32) * w_buf[t, r].astype(F32)).astype(BF)
        return carry

    lax.fori_loop(0, KB, multiply, 0)
    pl.semaphore_wait(barrier, (NZ - 1) + 15 + 8 + 1)

    for dy in (2, 1, 3, 0):
        for t in range(2):
            y_ = (y + dy) % NY
            pltpu.make_async_remote_copy(
                src_ref=product.at[t, :, pl.ds(pl.multiple_of(y_ * SUB, SUB), SUB)],
                dst_ref=cells.at[pl.ds(ka * KB, KB)],
                send_sem=p1_send,
                recv_sem=p1_recv,
                device_id=device(y_, 2 * ((core + t) % 2) + 1 - xl, z, t),
                device_id_type=MESH,
            ).start()

    to_core = pltpu.make_async_remote_copy(
        src_ref=column.at[:, pl.ds(KH * xl, KH)],
        dst_ref=cols.at[0, core],
        send_sem=col_send.at[0],
        recv_sem=col_recv.at[0],
        device_id=device(y, x, z, 1 - core),
        device_id_type=MESH,
    )
    to_x = pltpu.make_async_remote_copy(
        src_ref=column.at[:, pl.ds(KH * (1 - xl), KH)],
        dst_ref=cols.at[1, core],
        send_sem=col_send.at[1],
        recv_sem=col_recv.at[1],
        device_id=device(y, 2 * xh + 1 - xl, z, core),
        device_id_type=MESH,
    )
    forward = pltpu.make_async_remote_copy(
        src_ref=cols.at[1, core],
        dst_ref=cols.at[1, core],
        send_sem=col_send.at[2],
        recv_sem=col_recv.at[2],
        device_id=device(y, x, z, 1 - core),
        device_id_type=MESH,
    )
    to_core.start()

    first, second = placing_tables()
    placing[0:256] = first
    placing[256:512] = second

    def place(side, k):
        parts = [jnp.concatenate([cols[side, b, part, k] for b in range(2)], axis=0) for part in range(2)]
        both = jnp.concatenate(parts, axis=1)
        placed = lax.dot_general(
            placing[...], both, (((1,), (1,)), ((), ())), preferred_element_type=F32
        ).astype(BF)
        return jnp.concatenate([placed[0:256], placed[256:512]], axis=1)

    loads[3].wait()
    to_core.wait_recv()

    def place_own(k, carry):
        lhs[0, k] = place(0, k)
        return carry

    lax.fori_loop(0, KH, place_own, 0)
    to_x.start()
    loads[2].wait()

    pltpu.make_async_copy(cells, cells, p1_recv).wait()
    lattice_dft(cells, stage, spectral)

    place_of = (xh + core) % 2 * NY + y

    def send_points(chunk):
        start, count = STARTS[chunk], CHUNKS[chunk]
        pltpu.make_async_copy(
            spectral.at[:, pl.ds((ka * 2 + xl) * KH + start, count)], sigma[chunk].at[NA + place_of], p2_recv.at[chunk]
        ).start()
        for dy, dx in FAR_FIRST:
            y_, x_ = (y + dy) % NY, (x + dx) % NX
            pltpu.make_async_remote_copy(
                src_ref=spectral.at[:, pl.ds((y_ * NX + x_) * KH + start, count)],
                dst_ref=sigma[chunk].at[(1 + dx) % 2 * NA + place_of],
                send_sem=p2_send.at[chunk],
                recv_sem=p2_recv.at[chunk],
                device_id=device(y_, x_, z, core),
                device_id_type=MESH,
            ).start()

    for chunk in range(AHEAD):
        send_points(chunk)
        if chunk == AHEAD - 2:
            to_x.wait_recv()
            forward.start()
    forward.wait_recv()

    def band_of(chunk, kk, k):
        points = sigma[chunk]
        s = jnp.concatenate([points[:, part, kk].reshape(256, 128) for part in range(2)], axis=1)
        p_re, p_im = pan[0, k], pan[1, k]
        weights = jnp.concatenate(
            [jnp.concatenate([p_re, -p_im], axis=1), jnp.concatenate([p_im, p_re], axis=1)], axis=0
        )
        half = jnp.dot(s, weights, preferred_element_type=F32).astype(BF)
        stacked = jnp.concatenate(
            [half[0:128, 0:128], half[0:128, 128:256], half[128:256, 0:128], half[128:256, 128:256]], axis=0
        )
        rows = jnp.concatenate([lhs[0, k], place(1, k)], axis=1)
        return jnp.dot(rows, stacked, preferred_element_type=F32)

    def contract(chunk):
        start, count = STARTS[chunk], CHUNKS[chunk]
        for kk in range(count):
            to_send[start + kk] = band_of(chunk, kk, start + kk).astype(BF).reshape(NZ, 32, 128)
        for dz in (4, 3, 5, 2, 6, 1, 7):
            z_ = (z + dz) % NZ
            pltpu.make_async_remote_copy(
                src_ref=to_send.at[pl.ds(start, count), z_],
                dst_ref=received.at[z, pl.ds(start, count)],
                send_sem=r_send,
                recv_sem=r_recv.at[chunk],
                device_id=device(y, x, z_, core),
                device_id_type=MESH,
            ).start()

    def finish(chunk):
        start, count = STARTS[chunk], CHUNKS[chunk]
        some = received.at[pl.ds(0, NZ - 1), pl.ds(start, count)]
        pltpu.make_async_copy(some, some, r_recv.at[chunk]).wait()
        for k in range(start, start + count):
            total = to_send[k, z].astype(F32)
            for d in range(1, NZ):
                total = total + received[(z + d) % NZ, k].astype(F32)
            for g in range(4):
                quarter[g, k] = total[8 * g : 8 * g + 8]

        for d in range(1, 4):
            xl_, core_ = (xl + d // 2) % 2, (core + d % 2) % 2
            pltpu.make_async_remote_copy(
                src_ref=quarter.at[2 * xl_ + core_, pl.ds(start, count)],
                dst_ref=out.at[core, pl.ds(KH * xl + start, count)],
                send_sem=f_send,
                recv_sem=f_recv,
                device_id=device(y, 2 * xh + xl_, z, core_),
                device_id_type=MESH,
            ).start()
        out[core, pl.ds(KH * xl + start, count)] = quarter[2 * xl + core, pl.ds(start, count)]

    for chunk in range(LAST):
        if chunk + AHEAD <= LAST:
            send_points(chunk + AHEAD)
        pltpu.make_async_copy(sigma[chunk], sigma[chunk], p2_recv.at[chunk]).wait()
        contract(chunk)

    pltpu.make_async_copy(sigma[LAST], sigma[LAST], p2_recv.at[LAST]).wait()
    for kk in range(CHUNKS[LAST]):
        to_owner[:, kk] = band_of(LAST, kk, EARLY + kk).astype(BF).reshape(NZ * 2, 16, 128)
    for dz in (4, 3, 5, 2, 6, 1, 7, 0):
        for dx in (1, 0):
            if dz or dx:
                z_, xl_ = (z + dz) % NZ, (xl + dx) % 2
                pltpu.make_async_remote_copy(
                    src_ref=to_owner.at[z_ * 2 + xl_],
                    dst_ref=from_all.at[z * 2 + xl],
                    send_sem=l_send,
                    recv_sem=l_recv,
                    device_id=device(y, 2 * xh + xl_, z_, core),
                    device_id_type=MESH,
                ).start()
    from_all[z * 2 + xl] = to_owner[z * 2 + xl]

    for chunk in range(LAST):
        finish(chunk)

    most = from_all.at[pl.ds(0, 15)]
    pltpu.make_async_copy(most, most, l_recv).wait()
    for xl_ in range(2):
        for kk in range(CHUNKS[LAST]):
            total = from_all[xl_, kk].astype(F32)
            for z_ in range(1, NZ):
                total = total + from_all[2 * z_ + xl_, kk].astype(F32)
            for core_ in range(2):
                final[core_, xl_, kk] = total[8 * core_ : 8 * core_ + 8]
    for xl_ in range(2):
        pltpu.make_async_remote_copy(
            src_ref=final.at[1 - core, xl_],
            dst_ref=out.at[core, pl.ds(KH * xl_ + EARLY, CHUNKS[LAST])],
            send_sem=s_send,
            recv_sem=s_recv,
            device_id=device(y, x, z, 1 - core),
            device_id_type=MESH,
        ).start()
    for xl_ in range(2):
        out[core, pl.ds(KH * xl_ + EARLY, CHUNKS[LAST])] = final[core, xl_]

    three = quarter.at[pl.ds(0, 3)]
    pltpu.make_async_copy(three, three, f_recv).wait()

    pltpu.make_async_copy(cells, cells, p1_send).wait()
    to_core.wait_send()
    to_x.wait_send()
    forward.wait_send()
    for chunk in range(len(CHUNKS)):
        others = sigma[chunk].at[pl.ds(0, NY * NX - 1)]
        pltpu.make_async_copy(others, others, p2_send.at[chunk]).wait()
    others = received.at[pl.ds(0, NZ - 1)]
    pltpu.make_async_copy(others, others, r_send).wait()
    pltpu.make_async_copy(most, most, l_send).wait()
    pltpu.make_async_copy(three, three, f_send).wait()
    pltpu.make_async_copy(final.at[0], final.at[0], s_recv).wait()
    pltpu.make_async_copy(final.at[0], final.at[0], s_send).wait()


def body(green, screened, panel, column):
    dma = pltpu.SemaphoreType.DMA
    bands = pl.pallas_call(
        kernel,
        out_shape=jax.ShapeDtypeStruct((2, KB, 8, 128), F32),
        in_specs=[pl.BlockSpec(memory_space=pltpu.HBM)] * 4,
        out_specs=pl.BlockSpec(memory_space=pltpu.VMEM),
        scratch_shapes=[
            pltpu.VMEM((2, KB, 64, 128), BF),
            pltpu.VMEM((2, KB, 64, 128), BF),
            pltpu.VMEM((2, KB, 64, 128), BF),
            pltpu.VMEM((NK, SUB, 128), BF),
            pltpu.VMEM((LA, 24, SUB, 128), F32),
            pltpu.VMEM((2, NK, SUB, 128), BF),
            tuple(pltpu.VMEM((16, 2, count, SUB, 128), BF) for count in CHUNKS),
            pltpu.VMEM((2, KH, 128, 128), BF),
            pltpu.VMEM((2, 2, 2, KH, 64, 128), BF),
            pltpu.VMEM((512, 256), BF),
            pltpu.VMEM((1, KH, 256, 256), BF),
            pltpu.VMEM((EARLY, NZ, 32, 128), BF),
            pltpu.VMEM((NZ, EARLY, 32, 128), BF),
            pltpu.VMEM((4, EARLY, 8, 128), F32),
            pltpu.VMEM((NZ * 2, CHUNKS[LAST], 16, 128), BF),
            pltpu.VMEM((NZ * 2, CHUNKS[LAST], 16, 128), BF),
            pltpu.VMEM((2, 2, CHUNKS[LAST], 8, 128), F32),
            dma((3,)),
            dma,
            dma((3,)),
            dma((3,)),
            dma,
            dma,
            dma((len(CHUNKS),)),
            dma((len(CHUNKS),)),
            dma,
            dma((LAST,)),
            dma,
            dma,
            dma,
            dma,
            dma,
            dma,
        ],
        compiler_params=pltpu.CompilerParams(
            collective_id=0, has_side_effects=True, vmem_limit_bytes=int(53.5 * 1024) * 1024
        ),
    )(green, screened, panel, column)
    return jnp.transpose(bands.reshape(2, KB, 2, 4, 128), (0, 2, 1, 4, 3))


def solution(mesh):
    return jax.shard_map(
        body,
        mesh=mesh,
        in_specs=(
            P(None, "ka", "ta", None),
            P(None, "ka", "ta", None),
            P(None, "ka", None, None),
            P(None, "ka", "ta", None),
        ),
        out_specs=P(None, None, "ka", None, "ta"),
        check_vma=False,
    )
```

time: 54.7 us -> 48.4 us (0.88)
  Pallas kernels: 53 us -> 47.6 us
  local copies, waits for them, and re-layouts: 1.6 us -> 0.69 us
    pallas_call x1, Pallas kernels: 53 us -> 47.6 us  [body(): pl.pallas_call(kernel, out_shape=jax.ShapeDtypeStruct((2, KB, 8, 128), F3...]
    reshape x1, local copies, waits for them, and re-layouts: 1.6 us -> 0.69 us  [body(): return jnp.transpose(bands.reshape(2, KB, 2, 4, 128), (0, 2, 1, 4, 3))]
where the time goes in v2:
time: 48.4 us; the launch traced here: 48.3 us
  Pallas kernels  47.6 us (98%)
  local copies, waits for them, and re-layouts  0.69 us (1%)
    pallas_call x1, Pallas kernels, body(): pl.pallas_call(kernel, out_shape=jax.ShapeDtypeStruct((2, KB, 8, 128), F3...  47.6 us

profile of v2, /device:TPU:1, one launch (start us, length us, event | category | flops | bytes accessed | tf_op | source)
XLA Modules:
  0.0 48.3 jit_solution(6813315451483268466)
XLA Ops:
  0.0 47.6 %shard_map.46 = f32[2,18,8,128]{3,2,1,0:T(8,128)S(1)} custom-call(bf16[2,18,64,128]{3,2,1,0:T(8,128)(2,1)} %green.1, bf16[2,18,64,128]{3,2,1,0:T(8,128)(2,1)} %screened.1, bf16[2,18,128,128]{3,2,1,0:T(8,128)(2,1)} %panel.1, bf16[2,18,64,128]{3,2,1,0:T(8,128)(2,1)} %column.1), custom_call_target="tpu_custom_call" | custom-call | tf_op jit(solution)/shard_map/pallas_call | solution.py:384
  47.6 0.7 %copy.7 = f32[2,18,2,4,128]{4,3,1,2,0:T(4,128)} copy(f32[2,18,2,4,128]{4,3,2,1,0:T(4,128)S(1)} %bitcast.4) | data formatting | bytes 294912 | tf_op jit(solution)/shard_map/reshape | solution.py:428

commit v3 on v2

--- a/solution.py
+++ b/solution.py
@@ -14,7 +14,7 @@
 NK = 144
 KB = 18
 KH = 9
-CHUNKS = (2, 2, 2, 1, 2)
+CHUNKS = (2, 1, 2, 2, 2)
 STARTS = tuple(sum(CHUNKS[:i]) for i in range(len(CHUNKS)))
 LAST = len(CHUNKS) - 1
 EARLY = KH - CHUNKS[LAST]
@@ -341,6 +341,17 @@
         finish(chunk)
 
     most = from_all.at[pl.ds(0, 15)]
+    pltpu.make_async_copy(cells, cells, p1_send).wait()
+    to_core.wait_send()
+    to_x.wait_send()
+    forward.wait_send()
+    for chunk in range(len(CHUNKS)):
+        others = sigma[chunk].at[pl.ds(0, NY * NX - 1)]
+        pltpu.make_async_copy(others, others, p2_send.at[chunk]).wait()
+    others = received.at[pl.ds(0, NZ - 1)]
+    pltpu.make_async_copy(others, others, r_send).wait()
+    pltpu.make_async_copy(most, most, l_send).wait()
+
     pltpu.make_async_copy(most, most, l_recv).wait()
     for xl_ in range(2):
         for kk in range(CHUNKS[LAST]):
@@ -364,16 +375,6 @@
     three = quarter.at[pl.ds(0, 3)]
     pltpu.make_async_copy(three, three, f_recv).wait()
 
-    pltpu.make_async_copy(cells, cells, p1_send).wait()
-    to_core.wait_send()
-    to_x.wait_send()
-    forward.wait_send()
-    for chunk in range(len(CHUNKS)):
-        others = sigma[chunk].at[pl.ds(0, NY * NX - 1)]
-        pltpu.make_async_copy(others, others, p2_send.at[chunk]).wait()
-    others = received.at[pl.ds(0, NZ - 1)]
-    pltpu.make_async_copy(others, others, r_send).wait()
-    pltpu.make_async_copy(most, most, l_send).wait()
     pltpu.make_async_copy(three, three, f_send).wait()
     pltpu.make_async_copy(final.at[0], final.at[0], s_recv).wait()
     pltpu.make_async_copy(final.at[0], final.at[0], s_send).wait()

time: 48.4 us -> 48.5 us (level)
  no operation moved by 1% of the time
where the time goes in v3:
time: 48.5 us; the launch traced here: 48.4 us
  Pallas kernels  47.7 us (98%)
  local copies, waits for them, and re-layouts  0.69 us (1%)
    pallas_call x1, Pallas kernels, body(): pl.pallas_call(kernel, out_shape=jax.ShapeDtypeStruct((2, KB, 8, 128), F3...  47.7 us

profile of v3, /device:TPU:1, one launch (start us, length us, event | category | flops | bytes accessed | tf_op | source)
XLA Modules:
  0.0 48.4 jit_solution(2520441272822369102)
XLA Ops:
  0.0 47.7 %shard_map.46 = f32[2,18,8,128]{3,2,1,0:T(8,128)S(1)} custom-call(bf16[2,18,64,128]{3,2,1,0:T(8,128)(2,1)} %green.1, bf16[2,18,64,128]{3,2,1,0:T(8,128)(2,1)} %screened.1, bf16[2,18,128,128]{3,2,1,0:T(8,128)(2,1)} %panel.1, bf16[2,18,64,128]{3,2,1,0:T(8,128)(2,1)} %column.1), custom_call_target="tpu_custom_call" | custom-call | tf_op jit(solution)/shard_map/pallas_call | solution.py:385
  47.7 0.7 %copy.7 = f32[2,18,2,4,128]{4,3,1,2,0:T(4,128)} copy(f32[2,18,2,4,128]{4,3,2,1,0:T(4,128)S(1)} %bitcast.4) | data formatting | bytes 294912 | tf_op jit(solution)/shard_map/reshape | solution.py:429

commit v4 on v3

--- a/solution.py
+++ b/solution.py
@@ -18,6 +18,8 @@
 STARTS = tuple(sum(CHUNKS[:i]) for i in range(len(CHUNKS)))
 LAST = len(CHUNKS) - 1
 EARLY = KH - CHUNKS[LAST]
+SHY = 1
+PARTNER_LAST = [(dy, dx) for dx in (0, 1, 2, 3) for dy in (2, 1, 3, 0) if dy or dx]
 AHEAD = 3
 FAR_FIRST = sorted(
     ((dy, dx) for dy in range(NY) for dx in range(NX) if dy or dx),
@@ -73,8 +75,8 @@
     lax.fori_loop(0, LA, inner, 0)
 
     def put(k, re, im):
-        spectral[0, k] = re.astype(BF)
-        spectral[1, k] = im.astype(BF)
+        spectral[k, 0] = re.astype(BF)
+        spectral[k, 1] = im.astype(BF)
 
     def outer_complex(slot, k2, k3):
         re = [stage[r1, slot] for r1 in range(LA)]
@@ -139,6 +141,15 @@
     def device(y_, x_, z_, core_):
         return (y_ * 2 + x_ // 2, (x_ % 2 * NZ + z_) * 2 + core_)
 
+    loads = [
+        pltpu.make_async_copy(green, g_buf, load_sem.at[0]),
+        pltpu.make_async_copy(screened, w_buf, load_sem.at[1]),
+        pltpu.make_async_copy(panel.at[:, pl.ds(KH * xl, KH)], pan, load_sem.at[2]),
+        pltpu.make_async_copy(column.at[:, pl.ds(KH * xl, KH)], cols.at[0, core], col_local),
+    ]
+    loads[0].start()
+    loads[1].start()
+
     barrier = pltpu.get_barrier_semaphore()
 
     def greet(there):
@@ -153,21 +164,15 @@
     for dz in (4, 3, 5, 2, 6, 1, 7):
         greet(device(y, x, (z + dz) % NZ, core))
 
-    loads = [
-        pltpu.make_async_copy(green, g_buf, load_sem.at[0]),
-        pltpu.make_async_copy(screened, w_buf, load_sem.at[1]),
-        pltpu.make_async_copy(panel.at[:, pl.ds(KH * xl, KH)], pan, load_sem.at[2]),
-        pltpu.make_async_copy(column.at[:, pl.ds(KH * xl, KH)], cols.at[0, core], col_local),
-    ]
-    for load in loads:
-        load.start()
-
+    loads[2].start()
+    loads[3].start()
     loads[0].wait()
     loads[1].wait()
 
     def multiply(r, carry):
         for t in range(2):
-            product[t, r] = (g_buf[t, r].astype(F32) * w_buf[t, r].astype(F32)).astype(BF)
+            both = g_buf[t, r].astype(F32) * w_buf[t, r].astype(F32)
+            product[t, :, r] = both.astype(BF).reshape(NY, SUB, 128)
         return carry
 
     lax.fori_loop(0, KB, multiply, 0)
@@ -177,7 +182,7 @@
         for t in range(2):
             y_ = (y + dy) % NY
             pltpu.make_async_remote_copy(
-                src_ref=product.at[t, :, pl.ds(pl.multiple_of(y_ * SUB, SUB), SUB)],
+                src_ref=product.at[t, y_],
                 dst_ref=cells.at[pl.ds(ka * KB, KB)],
                 send_sem=p1_send,
                 recv_sem=p1_recv,
@@ -226,12 +231,13 @@
     loads[3].wait()
     to_core.wait_recv()
 
+    to_x.start()
+
     def place_own(k, carry):
         lhs[0, k] = place(0, k)
         return carry
 
     lax.fori_loop(0, KH, place_own, 0)
-    to_x.start()
     loads[2].wait()
 
     pltpu.make_async_copy(cells, cells, p1_recv).wait()
@@ -242,12 +248,13 @@
     def send_points(chunk):
         start, count = STARTS[chunk], CHUNKS[chunk]
         pltpu.make_async_copy(
-            spectral.at[:, pl.ds((ka * 2 + xl) * KH + start, count)], sigma[chunk].at[NA + place_of], p2_recv.at[chunk]
+            spectral.at[pl.ds((ka * 2 + xl) * KH + start, count)], sigma[chunk].at[NA + place_of], p2_recv.at[chunk]
         ).start()
-        for dy, dx in FAR_FIRST:
-            y_, x_ = (y + dy) % NY, (x + dx) % NX
+        for dy, dx in PARTNER_LAST if chunk < SHY else FAR_FIRST:
+            y_ = (y + dy) % NY
+            x_ = (x + (NX - dx + 2 * dx * xl if chunk < SHY else dx)) % NX
             pltpu.make_async_remote_copy(
-                src_ref=spectral.at[:, pl.ds((y_ * NX + x_) * KH + start, count)],
+                src_ref=spectral.at[pl.ds((y_ * NX + x_) * KH + start, count)],
                 dst_ref=sigma[chunk].at[(1 + dx) % 2 * NA + place_of],
                 send_sem=p2_send.at[chunk],
                 recv_sem=p2_recv.at[chunk],
@@ -264,7 +271,7 @@
 
     def band_of(chunk, kk, k):
         points = sigma[chunk]
-        s = jnp.concatenate([points[:, part, kk].reshape(256, 128) for part in range(2)], axis=1)
+        s = jnp.concatenate([points[:, kk, part].reshape(256, 128) for part in range(2)], axis=1)
         p_re, p_im = pan[0, k], pan[1, k]
         weights = jnp.concatenate(
             [jnp.concatenate([p_re, -p_im], axis=1), jnp.concatenate([p_im, p_re], axis=1)], axis=0
@@ -273,7 +280,8 @@
         stacked = jnp.concatenate(
             [half[0:128, 0:128], half[0:128, 128:256], half[128:256, 0:128], half[128:256, 128:256]], axis=0
         )
-        rows = jnp.concatenate([lhs[0, k], place(1, k)], axis=1)
+        other = lhs[1, k] if chunk == LAST else place(1, k)
+        rows = jnp.concatenate([lhs[0, k], other], axis=1)
         return jnp.dot(rows, stacked, preferred_element_type=F32)
 
     def contract(chunk):
@@ -320,6 +328,8 @@
         pltpu.make_async_copy(sigma[chunk], sigma[chunk], p2_recv.at[chunk]).wait()
         contract(chunk)
 
+    for k in range(EARLY, KH):
+        lhs[1, k] = place(1, k)
     pltpu.make_async_copy(sigma[LAST], sigma[LAST], p2_recv.at[LAST]).wait()
     for kk in range(CHUNKS[LAST]):
         to_owner[:, kk] = band_of(LAST, kk, EARLY + kk).astype(BF).reshape(NZ * 2, 16, 128)
@@ -390,15 +400,15 @@
         scratch_shapes=[
             pltpu.VMEM((2, KB, 64, 128), BF),
             pltpu.VMEM((2, KB, 64, 128), BF),
-            pltpu.VMEM((2, KB, 64, 128), BF),
+            pltpu.VMEM((2, NY, KB, SUB, 128), BF),
             pltpu.VMEM((NK, SUB, 128), BF),
             pltpu.VMEM((LA, 24, SUB, 128), F32),
-            pltpu.VMEM((2, NK, SUB, 128), BF),
-            tuple(pltpu.VMEM((16, 2, count, SUB, 128), BF) for count in CHUNKS),
+            pltpu.VMEM((NK, 2, SUB, 128), BF),
+            tuple(pltpu.VMEM((16, count, 2, SUB, 128), BF) for count in CHUNKS),
             pltpu.VMEM((2, KH, 128, 128), BF),
             pltpu.VMEM((2, 2, 2, KH, 64, 128), BF),
             pltpu.VMEM((512, 256), BF),
-            pltpu.VMEM((1, KH, 256, 256), BF),
+            pltpu.VMEM((2, KH, 256, 256), BF),
             pltpu.VMEM((EARLY, NZ, 32, 128), BF),
             pltpu.VMEM((NZ, EARLY, 32, 128), BF),
             pltpu.VMEM((4, EARLY, 8, 128), F32),

time: 48.5 us -> 48.5 us (level)
  no operation moved by 1% of the time
where the time goes in v4:
time: 48.5 us; the launch traced here: 48.4 us
  Pallas kernels  47.7 us (98%)
  local copies, waits for them, and re-layouts  0.69 us (1%)
    pallas_call x1, Pallas kernels, body(): pl.pallas_call(kernel, out_shape=jax.ShapeDtypeStruct((2, KB, 8, 128), F3...  47.7 us

profile of v4, /device:TPU:1, one launch (start us, length us, event | category | flops | bytes accessed | tf_op | source)
XLA Modules:
  0.0 48.4 jit_solution(5621535741908690139)
XLA Ops:
  0.0 47.7 %shard_map.46 = f32[2,18,8,128]{3,2,1,0:T(8,128)S(1)} custom-call(bf16[2,18,64,128]{3,2,1,0:T(8,128)(2,1)} %green.1, bf16[2,18,64,128]{3,2,1,0:T(8,128)(2,1)} %screened.1, bf16[2,18,128,128]{3,2,1,0:T(8,128)(2,1)} %panel.1, bf16[2,18,64,128]{3,2,1,0:T(8,128)(2,1)} %column.1), custom_call_target="tpu_custom_call" | custom-call | tf_op jit(solution)/shard_map/pallas_call | solution.py:395
  47.7 0.7 %copy.7 = f32[2,18,2,4,128]{4,3,1,2,0:T(4,128)} copy(f32[2,18,2,4,128]{4,3,2,1,0:T(4,128)S(1)} %bitcast.4) | data formatting | bytes 294912 | tf_op jit(solution)/shard_map/reshape | solution.py:439
